TPU v7x, 256 devices: a whole 4x4x8 slice. The times are simulated.
256 devices in a mesh: group: 32 (over z, x), head: 8 (over y, core).
Axes of the slice: x: 4, y: 4, z: 8, core: 2. Of those that a mesh axis runs over, the one named last changes fastest.
Arguments:
- noisy_qkv: bfloat16 [32768, 3, 3072], P(('group', 'head')), may hold values from -8 to 8
- clean_kv: bfloat16 [32768, 2, 3072], P('group', None, 'head'), may hold values from -8 to 8
- video_lengths: int32 [4], replicated, may hold values from 1 to 20, 32 in all
- pattern: int32 [4, 4], replicated, may hold values 0 or 1
Outputs:
- attended: bfloat16 [32768, 3072], P(('group', 'head'))
Inputs may be any that keep to these rules, and one draw needn't show every extreme that they name: `video_lengths`: the largest entry is exactly 20.
All inputs are finite; a program needn't handle non-finite values.
Results may differ from a plain program's by a relative error of at most 0.0065.
Values may be sent and summed in bfloat16 or wider, within the bound.
A program may use at most 192 MiB of HBM per device.

v0:
```python
import jax
import jax.numpy as jnp
from jax import lax
from jax.sharding import PartitionSpec as P

HEAD_DIM = 128
REACH = 4


def passed_along(block, axis, distance):
    devices = range(lax.axis_size(axis))
    route = [(i - distance, i) for i in devices if i - distance in devices]
    return lax.ppermute(block, axis, route)


def block_scores(query, keys, scale):
    return jnp.einsum("qhd,khd->hqk", query, keys, preferred_element_type=jnp.float32) * scale


def on_device(noisy_qkv, clean_kv, video_lengths, pattern):
    local = lax.all_to_all(noisy_qkv, "head", split_axis=2, concat_axis=0, tiled=True)
    tokens = local.shape[0]
    width = local.shape[2]
    heads_here = width // HEAD_DIM
    split = local.reshape(tokens, 3, heads_here, HEAD_DIM)
    query = split[:, 0]
    scale = HEAD_DIM ** (-0.5)
    group_index = lax.axis_index("group")
    ends = jnp.cumsum(video_lengths)
    video = jnp.sum((ends <= group_index).astype(jnp.int32))
    picked = jnp.arange(ends.shape[0], dtype=jnp.int32) == video
    first = jnp.sum(jnp.where(picked, ends - video_lengths, 0))
    row = jnp.sum(jnp.where(picked[:, None], pattern, 0), axis=0)
    blocks = []
    current = clean_kv
    for step in range(REACH):
        current = passed_along(current, "group", 1)
        blocks.append(current)
    scores = block_scores(query, split[:, 1], scale)
    running = jnp.max(scores, axis=2)
    expo = jnp.exp(scores - running[:, :, None])
    total = jnp.sum(expo, axis=2)
    accum = jnp.einsum(
        "hqk,khd->qhd", expo.astype(jnp.bfloat16), split[:, 2], preferred_element_type=jnp.float32
    )
    for step in range(REACH):
        block = blocks[step].reshape(tokens, 2, heads_here, HEAD_DIM)
        keep = (group_index - (step + 1) >= first) & (row[step] == 1)
        scores = block_scores(query, block[:, 0], scale)
        block_max = jnp.where(keep, jnp.max(scores, axis=2), running)
        new_max = jnp.maximum(running, block_max)
        factor = jnp.exp(running - new_max)
        expo = jnp.where(keep, jnp.exp(scores - new_max[:, :, None]), 0.0)
        total = total * factor + jnp.sum(expo, axis=2)
        added = jnp.einsum(
            "hqk,khd->qhd",
            expo.astype(jnp.bfloat16),
            block[:, 1],
            preferred_element_type=jnp.float32,
        )
        accum = accum * jnp.transpose(factor)[:, :, None] + added
        running = new_max
    result = accum / jnp.transpose(total)[:, :, None]
    result = result.astype(jnp.bfloat16).reshape(tokens, width)
    return lax.all_to_all(result, "head", split_axis=0, concat_axis=1, tiled=True)


def solution(mesh):
    return jax.shard_map(
        on_device,
        mesh=mesh,
        in_specs=(P(("group", "head"), None, None), P("group", None, "head"), P(), P()),
        out_specs=P(("group", "head"), None),
        check_vma=False,
    )
```

profile of v0, /device:TPU:128, one launch (start us, length us, event | category | flops | bytes accessed | tf_op | source)
XLA Modules:
  0.0 241.1 jit_solution(6655610851805472739)
XLA Ops:
  0.0 5.0 %copy.56 = bf16[1024,2,384]{0,2,1:T(8,128)(2,1)} copy(bf16[1024,2,384]{2,1,0:T(2,128)(2,1)} %param.5) | data formatting | bytes 3145728 | tf_op args[1]
  5.0 3.4 %collective-permute-start = (bf16[1024,2,384]{0,2,1:T(8,128)(2,1)}, bf16[1024,2,384]{0,2,1:T(8,128)(2,1)}, u32[]{:S(2)}, u32[]{:S(2)}) collective-permute-start(bf16[1024,2,384]{0,2,1:T(8,128)(2,1)} %copy.56), channel_id=1, source_target_pairs={{0,8},{8,16},{16,24},{24,32},{32,40},{40,48},{48,56},{56,64},{64,7... | collective-permute-start | bytes 4718600 | tf_op jit(solution)/shard_map/ppermute | solution.py:13
  8.4 5.7 %copy.50 = bf16[128,3,3072]{0,1,2:T(4,128)(2,1)} copy(bf16[128,3,3072]{2,0,1:T(8,128)(2,1)} %param.4) | data formatting | bytes 4718592 | tf_op args[0]
  14.1 4.5 %all-to-all-start = ((bf16[128,3,3072]{0,1,2:T(4,128)(2,1)}), bf16[128,3,3072]{0,1,2:T(4,128)(2,1)S(1)}, u32[]{:S(2)}, u32[]{:S(2)}) async-start(bf16[128,3,3072]{0,1,2:T(4,128)(2,1)} %copy.50), calls=%async_computation | async-start | bytes 6291456 | tf_op jit(solution)/shard_map/all_to_all | solution.py:21
  18.5 28.1 %collective-permute-done = bf16[1024,2,384]{0,2,1:T(8,128)(2,1)} collective-permute-done((bf16[1024,2,384]{0,2,1:T(8,128)(2,1)}, bf16[1024,2,384]{0,2,1:T(8,128)(2,1)}, u32[]{:S(2)}, u32[]{:S(2)}) %collective-permute-start) | collective-permute-done | bytes 1572896 | tf_op jit(solution)/shard_map/ppermute | solution.py:13
  46.6 1.9 collective-permute-start.1
  49.4 1.2 fusion.45
  52.8 0.7 iota_compare_fusion
  53.5 0.7 fusion.57
  57.0 3.3 %copy.90 = bf16[128,3,8,384]{0,2,3,1:T(8,128)(2,1)} copy(bf16[128,3,8,384]{0,1,3,2:T(4,128)(2,1)S(1)} %bitcast.192) | data formatting | bytes 4718592 | tf_op jit(solution)/shard_map/all_to_all | solution.py:21
  60.3 5.0 %reshape.101 = bf16[1024,3,3,128]{0,3,2,1:T(8,128)(2,1)} reshape(bf16[8,128,3,384]{1,0,3,2:T(8,128)(2,1)} %bitcast.193) | data formatting | bytes 4718592 | tf_op jit(solution)/shard_map/reshape | solution.py:25
  65.2 22.2 %collective-permute-done.1 = bf16[1024,2,384]{0,2,1:T(8,128)(2,1)} collective-permute-done((bf16[1024,2,384]{0,2,1:T(8,128)(2,1)}, bf16[1024,2,384]{0,2,1:T(8,128)(2,1)}, u32[]{:S(2)}, u32[]{:S(2)}) %collective-permute-start.1) | collective-permute-done | bytes 1572896 | tf_op jit(solution)/shard_map/ppermute | solution.py:13
  87.4 1.9 collective-permute-start.2
  89.3 3.2 %multiply_reduce_fusion.4 = (f32[3,1024]{1,0:T(4,128)S(1)}, f32[3,1024,1024]{1,2,0:T(8,128)S(1)}) fusion(bf16[1024,3,3,128]{0,3,2,1:T(8,128)(2,1)} %reshape.101), kind=kOutput, calls=%fused_computation.9 | convolution fusion | flops 811594752 | bytes 14168064 | tf_op jit(solution)/shard_map/qhd,khd->hqk/dot_general | solution.py:17
  92.5 2.1 fusion
  94.6 4.1 %fusion.10 = f32[3,1024,128]{2,1,0:T(8,128)S(1)} fusion(f32[3,1024,1024]{1,2,0:T(8,128)S(1)} %get-tuple-element.25, f32[3,1024]{1,0:T(4,128)S(1)} %get-tuple-element.24, bf16[1024,3,3,128]{0,3,2,1:T(8,128)(2,1)} %reshape.101), kind=kOutput, calls=%fused_computation.20 | convolution fusion | flops 814743552 | bytes 14954496 | tf_op jit(solution)/shard_map/hqk,khd->qhd/dot_general | solution.py:43
  98.7 28.6 %collective-permute-done.2 = bf16[1024,2,384]{0,2,1:T(8,128)(2,1)} collective-permute-done((bf16[1024,2,384]{0,2,1:T(8,128)(2,1)}, bf16[1024,2,384]{0,2,1:T(8,128)(2,1)}, u32[]{:S(2)}, u32[]{:S(2)}) %collective-permute-start.2) | collective-permute-done | bytes 1572896 | tf_op jit(solution)/shard_map/ppermute | solution.py:13
  127.3 2.1 collective-permute-start.3
  129.4 7.7 %multiply_reduce_fusion.3 = (f32[3,1024]{1,0:T(4,128)S(1)}, f32[3,1024,1024]{1,2,0:T(8,128)}) fusion(bf16[1024,2,3,128]{0,3,2,1:T(8,128)(2,1)} %bitcast.10, bf16[1024,3,3,128]{0,3,2,1:T(8,128)(2,1)} %reshape.101), kind=kOutput, calls=%fused_computation.8 | convolution fusion | flops 811594752 | bytes 14168064 | tf_op jit(solution)/shard_map/qhd,khd->hqk/dot_general | solution.py:17
  137.0 7.6 %multiply_reduce_fusion.2 = (f32[3,1024]{1,0:T(4,128)S(1)}, f32[3,1024,1024]{1,2,0:T(8,128)}) fusion(bf16[1024,2,3,128]{0,3,2,1:T(8,128)(2,1)} %bitcast.16, bf16[1024,3,3,128]{0,3,2,1:T(8,128)(2,1)S(1)} %copy-done), kind=kOutput, calls=%fused_computation.7 | convolution fusion | flops 811594752 | bytes 14168064 | tf_op jit(solution)/shard_map/qhd,khd->hqk/dot_general | solution.py:17
  144.6 7.5 %multiply_reduce_fusion.1 = (f32[3,1024]{1,0:T(4,128)S(1)}, f32[3,1024,1024]{1,2,0:T(8,128)}) fusion(bf16[1024,2,3,128]{0,3,2,1:T(8,128)(2,1)} %bitcast.22, bf16[1024,3,3,128]{0,3,2,1:T(8,128)(2,1)S(1)} %copy-done), kind=kOutput, calls=%fused_computation.6 | convolution fusion | flops 811594752 | bytes 14168064 | tf_op jit(solution)/shard_map/qhd,khd->hqk/dot_general | solution.py:17
  152.1 14.0 %collective-permute-done.3 = bf16[1024,2,384]{0,2,1:T(8,128)(2,1)S(1)} collective-permute-done((bf16[1024,2,384]{0,2,1:T(8,128)(2,1)}, bf16[1024,2,384]{0,2,1:T(8,128)(2,1)S(1)}, u32[]{:S(2)}, u32[]{:S(2)}) %collective-permute-start.3) | collective-permute-done | bytes 1572896 | tf_op jit(solution)/shard_map/ppermute | solution.py:13
  166.1 1.8 multiply_reduce_fusion
  168.0 9.2 %fusion.18 = f32[3,1024,128]{2,1,0:T(8,128)} fusion(f32[3,1024,1024]{1,2,0:T(8,128)} %get-tuple-element.23, f32[3,1024]{1,0:T(4,128)S(1)} %get-tuple-element.12, pred[]{:T(512)S(6)} %and.14, bf16[1024,2,3,128]{0,3,2,1:T(8,128)(2,1)} %bitcast.16), kind=kOutput, calls=%fused_computation.25 | convolution fusion | flops 817889280 | bytes 14954497 | tf_op jit(solution)/shard_map/hqk,khd->qhd/dot_general | solution.py:55
  177.2 10.5 %fusion.2 = (f32[3,1024]{1,0:T(4,128)S(1)}, f32[3,1024]{1,0:T(4,128)S(1)}) fusion(f32[3,1024,1024]{1,2,0:T(8,128)} %get-tuple-element.27, f32[3,1024]{1,0:T(4,128)S(1)} %get-tuple-element.13, pred[]{:T(512)S(6)} %and.13, f32[3,1024]{1,0:T(4,128)S(1)} %get-tuple-element.12, f32[3,1024,1024]{1,2,0:T(8,128)} %get-tuple-element.23, pred[]{:T(512)S(6)} %and.14), kind=kLoop, calls=%fused_computation.12 | loop fusion | flops 25159680 | bytes 25214978 | tf_op jit(solution)/shard_map/reduce_sum | solution.py:54
  187.8 9.2 %fusion.20 = f32[3,1024,128]{2,1,0:T(8,128)} fusion(f32[3,1024,1024]{1,2,0:T(8,128)} %get-tuple-element.27, f32[3,1024]{1,0:T(4,128)S(1)} %get-tuple-element.13, pred[]{:T(512)S(6)} %and.13, bf16[1024,2,3,128]{0,3,2,1:T(8,128)(2,1)} %bitcast.10), kind=kOutput, calls=%fused_computation.26 | convolution fusion | flops 817889280 | bytes 14954497 | tf_op jit(solution)/shard_map/hqk,khd->qhd/dot_general | solution.py:55
  197.0 9.2 %fusion.16 = f32[3,1024,128]{2,1,0:T(8,128)} fusion(f32[3,1024,1024]{1,2,0:T(8,128)} %get-tuple-element.21, f32[3,1024]{1,0:T(4,128)S(1)} %get-tuple-element.11, pred[]{:T(512)S(6)} %and.15, bf16[1024,2,3,128]{0,3,2,1:T(8,128)(2,1)} %bitcast.22), kind=kOutput, calls=%fused_computation.24 | convolution fusion | flops 817889280 | bytes 14954497 | tf_op jit(solution)/shard_map/hqk,khd->qhd/dot_general | solution.py:55
  206.2 8.1 %fusion.6 = (f32[3,1024]{1,0:T(4,128)S(1)}, f32[3,1024]{1,0:T(4,128)S(1)}) fusion(f32[3,1024,1024]{1,2,0:T(8,128)} %get-tuple-element.21, f32[3,1024]{1,0:T(4,128)S(1)} %get-tuple-element.11, pred[]{:T(512)S(6)} %and.15, f32[3,1024]{1,0:T(4,128)S(1)} %get-tuple-element.10, f32[3,1024,1024]{1,2,0:T(8,128)S(1)} %get-tuple-element.19, pred[]{:T(512)S(6)} %and.16), kind=kLoop, calls=%fused_computation.16 | loop fusion | flops 25159680 | bytes 25214978 | tf_op jit(solution)/shard_map/reduce_sum | solution.py:54
  214.5 6.2 %fusion.27 = bf16[1024,3,128]{2,0,1:T(8,128)(2,1)} fusion(f32[3,1024,128]{2,1,0:T(8,128)S(1)} %copy-done.7, f32[3,1024,128]{2,1,0:T(8,128)S(1)} %copy-done.5, f32[3,1024,128]{2,1,0:T(8,128)S(1)} %copy-done.6, f32[3,1024,128]{2,1,0:T(8,128)S(1)} %fusion.10, f32[3,1024,1024]{1,2,0:T(8,128)S(1)} %get-tuple-element.19, f32[3,1024]{1,0:T(4,128)S(1)} %get-tuple-element.10, ...), kind=kOutput, calls=%fused_computation.34 | convolution fusion | flops 821821440 | bytes 20545536 | tf_op jit(solution)/shard_map/hqk,khd->qhd/dot_general | solution.py:55
  220.7 1.4 copy.69
  222.4 17.5 %all_to_all.34 = bf16[8,128,384]{1,2,0:T(8,128)(2,1)S(1)} all-to-all(bf16[8,128,384]{1,2,0:T(8,128)(2,1)S(1)} %copy.70), channel_id=1, replica_groups=mesh['group'=32,'head'=8] {'head'}, dimensions={0} | all-to-all | bytes 1572864 | tf_op jit(solution)/shard_map/all_to_all | solution.py:65
  239.9 1.2 copy.71
  (24 shorter events, 1.5 us)
Async XLA Ops:
  0.0 48.5 %copy-start.4 = (s32[4]{0:T(128)S(1)}, s32[4]{0:T(128)}, u32[]{:S(2)}) copy-start(s32[4]{0:T(128)} %param.6) | copy-start | bytes 52
  0.0 53.5 %copy-start.3 = (s32[4,4]{1,0:T(4,128)S(1)}, s32[4,4]{1,0:T(4,128)}, u32[]{:S(2)}) copy-start(s32[4,4]{1,0:T(4,128)} %param.7) | copy-start | bytes 196
  5.0 41.7 %collective-permute-start = (bf16[1024,2,384]{0,2,1:T(8,128)(2,1)}, bf16[1024,2,384]{0,2,1:T(8,128)(2,1)}, u32[]{:S(2)}, u32[]{:S(2)}) collective-permute-start(bf16[1024,2,384]{0,2,1:T(8,128)(2,1)} %copy.56), channel_id=1, source_target_pairs={{0,8},{8,16},{16,24},{24,32},{32,40},{40,48},{48,56},{56,64},{64,7... | collective-permute-start | bytes 4718600 | tf_op jit(solution)/shard_map/ppermute | solution.py:13
  14.1 42.9 %all-to-all-start = ((bf16[128,3,3072]{0,1,2:T(4,128)(2,1)}), bf16[128,3,3072]{0,1,2:T(4,128)(2,1)S(1)}, u32[]{:S(2)}, u32[]{:S(2)}) async-start(bf16[128,3,3072]{0,1,2:T(4,128)(2,1)} %copy.50), calls=%async_computation | async-start | bytes 6291456 | tf_op jit(solution)/shard_map/all_to_all | solution.py:21
  46.6 40.8 %collective-permute-start.1 = (bf16[1024,2,384]{0,2,1:T(8,128)(2,1)}, bf16[1024,2,384]{0,2,1:T(8,128)(2,1)}, u32[]{:S(2)}, u32[]{:S(2)}) collective-permute-start(bf16[1024,2,384]{0,2,1:T(8,128)(2,1)} %collective-permute-done), channel_id=1, source_target_pairs={{0,8},{8,16},{16,24},{24,32},{32,40},{40,48},{48,56},{56,64},{64,7... | collective-permute-start | bytes 4718600 | tf_op jit(solution)/shard_map/ppermute | solution.py:13
  87.4 39.9 %collective-permute-start.2 = (bf16[1024,2,384]{0,2,1:T(8,128)(2,1)}, bf16[1024,2,384]{0,2,1:T(8,128)(2,1)}, u32[]{:S(2)}, u32[]{:S(2)}) collective-permute-start(bf16[1024,2,384]{0,2,1:T(8,128)(2,1)} %collective-permute-done.1), channel_id=1, source_target_pairs={{0,8},{8,16},{16,24},{24,32},{32,40},{40,48},{48,56},{56,64},{64,7... | collective-permute-start | bytes 4718600 | tf_op jit(solution)/shard_map/ppermute | solution.py:13
  98.7 38.4 %copy-start = (bf16[1024,3,3,128]{0,3,2,1:T(8,128)(2,1)S(1)}, bf16[1024,3,3,128]{0,3,2,1:T(8,128)(2,1)}, u32[]{:S(2)}) copy-start(bf16[1024,3,3,128]{0,3,2,1:T(8,128)(2,1)} %reshape.101) | copy-start | bytes 7077892
  127.3 38.8 %collective-permute-start.3 = (bf16[1024,2,384]{0,2,1:T(8,128)(2,1)}, bf16[1024,2,384]{0,2,1:T(8,128)(2,1)S(1)}, u32[]{:S(2)}, u32[]{:S(2)}) collective-permute-start(bf16[1024,2,384]{0,2,1:T(8,128)(2,1)} %collective-permute-done.2), channel_id=1, source_target_pairs={{0,8},{8,16},{16,24},{24,32},{32,40},{40,48},{48,56},{56,64},{64,7... | collective-permute-start | bytes 4718600 | tf_op jit(solution)/shard_map/ppermute | solution.py:13
  166.1 1.9 copy-start.1
  206.2 8.2 %copy-start.2 = (bf16[1024,2,384]{0,2,1:T(8,128)(2,1)S(1)}, bf16[1024,2,384]{0,2,1:T(8,128)(2,1)}, u32[]{:S(2)}) copy-start(bf16[1024,2,384]{0,2,1:T(8,128)(2,1)} %copy-done.1) | copy-start | bytes 4718596
  206.2 8.2 %copy-start.5 = (f32[3,1024,128]{2,1,0:T(8,128)S(1)}, f32[3,1024,128]{2,1,0:T(8,128)}, u32[]{:S(2)}) copy-start(f32[3,1024,128]{2,1,0:T(8,128)} %fusion.18) | copy-start | bytes 4718596
  206.2 8.2 %copy-start.6 = (f32[3,1024,128]{2,1,0:T(8,128)S(1)}, f32[3,1024,128]{2,1,0:T(8,128)}, u32[]{:S(2)}) copy-start(f32[3,1024,128]{2,1,0:T(8,128)} %fusion.20) | copy-start | bytes 4718596
  206.2 8.2 %copy-start.7 = (f32[3,1024,128]{2,1,0:T(8,128)S(1)}, f32[3,1024,128]{2,1,0:T(8,128)}, u32[]{:S(2)}) copy-start(f32[3,1024,128]{2,1,0:T(8,128)} %fusion.16) | copy-start | bytes 4718596
where the time goes:
time: 242 us; the launch traced here: 241 us
  waiting for transfers between devices  93 us (38%)
  matrix products  65.8 us (27%)
  other arithmetic  23.6 us (10%)
  local copies, waits for them, and re-layouts  22.5 us (9%)
  blocking collectives  17.5 us (7%)
  starting transfers between devices  13.8 us (6%)
  between operations  4.94 us (2%)
    ppermute x4, waiting for transfers between devices, passed_along(): return lax.ppermute(block, axis, route)  92.8 us
    dot_general x4, matrix products, on_device(): jnp.einsum('hqk,khd->qhd', expo.astype(jnp.bfloat16), block[:, 1], prefer...  33.9 us
    dot_general x5, matrix products, block_scores(): jnp.einsum('qhd,khd->hqk', query, keys, preferred_element_type=jnp.float32)  27.8 us
    reduce_sum x2, other arithmetic, on_device(): total = total * factor + jnp.sum(expo, axis=2)  18.7 us
    all_to_all x1, blocking collectives, on_device(): lax.all_to_all(result, 'head', split_axis=0, concat_axis=1, tiled=True)  17.5 us
    unnamed x19, local copies, waits for them, and re-layouts  10.9 us
    ppermute x4, starting transfers between devices, passed_along(): return lax.ppermute(block, axis, route)  9.3 us
    reshape x1, local copies, waits for them, and re-layouts, on_device(): split = local.reshape(tokens, 3, heads_here, HEAD_DIM)  4.96 us
  transfers between devices with their start and end apart: 5, of which 5 were waited for; matrix products, arithmetic and copies ran while one was open for 21% of the time, Pallas kernels for 0%

commit v1 on v0

v1 whole, which is shorter than its diff:
```python
import functools

import jax
import jax.numpy as jnp
from jax import lax
from jax.experimental import pallas as pl
from jax.experimental.pallas import tpu as pltpu
from jax.sharding import PartitionSpec as P

MESH = pl.DeviceIdType.MESH
HEAD_DIM = 128
REACH = 4
ROW = 4
EXP2_SCALE = HEAD_DIM ** (-0.5) * 1.4426950408889634
FAR = 1e30

NOISY, OWN, ABOVE, ACROSS = 0, 1, 2, 3
MINE, PARTNER = 0, 1

STEPS = (
    (ABOVE, MINE, 0),
    (ACROSS, MINE, 0),
    (None, PARTNER, 0),
    (ACROSS, PARTNER, 0),
    (NOISY, MINE, 0),
    (ABOVE, MINE, 1),
    (NOISY, MINE, 1),
    (None, PARTNER, 1),
    (ACROSS, PARTNER, 1),
    (ACROSS, MINE, 1),
    (ABOVE, MINE, 2),
    (NOISY, MINE, 2),
    (None, PARTNER, 2),
    (ACROSS, PARTNER, 2),
    (ACROSS, MINE, 2),
)


def lookup(step, values):
    out = jnp.int32(values[0])
    for i, value in enumerate(values):
        if i and value != values[0]:
            out = jnp.where(step == i, jnp.int32(value), out)
    return out


def validity(group, lengths_ref, pattern_ref):
    videos = lengths_ref.shape[0]
    video, end = jnp.int32(0), jnp.int32(0)
    starts = []
    for j in range(videos):
        starts.append(end)
        end = end + lengths_ref[j]
        video = video + jnp.where(end <= group, 1, 0)
    first = jnp.int32(0)
    row = [jnp.int32(0)] * REACH
    for j in range(videos):
        first = jnp.where(video == j, starts[j], first)
        row = [jnp.where(video == j, pattern_ref[j, h], row[h]) for h in range(REACH)]
    return [(group - (h + 1) >= first) & (row[h] == 1) for h in range(REACH)]


def kernel(
    groups, heads_axis,
    noisy_ref, clean_ref, lengths_ref, pattern_ref, out_ref,
    query, keyval, accum, peak, total, part, part_stat, got, got_stat, final,
    noisy_send, noisy_recv, clean_send, clean_recv, query_send, query_recv,
    part_send, part_recv, out_send, out_recv, local_sem,
):
    group, head = lax.axis_index("group"), lax.axis_index("head")
    rows = noisy_ref.shape[1]
    width = keyval.shape[3]
    heads_here = width // HEAD_DIM
    column = lax.rem(group, ROW)
    odd = lax.rem(column, 2)
    near = group + 1 - 2 * odd
    far = group - column + (ROW - 1) - column
    below = lax.rem(group + ROW, groups)
    above = lax.rem(group + groups - ROW, groups)
    peers = [lax.rem(head + k, heads_axis) for k in range(1, heads_axis)]

    mine_ok = validity(group, lengths_ref, pattern_ref)
    near_ok = validity(near, lengths_ref, pattern_ref)

    def remote(src, dst, send, recv, to_group, to_head):
        return pltpu.make_async_remote_copy(
            src_ref=src, dst_ref=dst, send_sem=send, recv_sem=recv,
            device_id=(to_group, to_head), device_id_type=MESH,
        )

    def columns(index):
        return pl.ds(pl.multiple_of(index * width, width), width)

    def lanes(h):
        return pl.ds(h * HEAD_DIM, HEAD_DIM)

    my_rows = pl.ds(pl.multiple_of(head * rows, rows), rows)

    def noisy_target(which):
        return query.at[MINE] if which == 0 else keyval.at[NOISY, which - 1]

    def noisy_copy(which, k):
        to = peers[k]
        return remote(
            noisy_ref.at[which, :, columns(to)], noisy_target(which).at[my_rows, :],
            noisy_send.at[which, k], noisy_recv.at[which, k], group, to,
        )

    def noisy_local(which):
        return pltpu.make_async_copy(
            noisy_ref.at[which, :, columns(head)], noisy_target(which).at[my_rows, :], local_sem.at[which]
        )

    def own_copy(which):
        return pltpu.make_async_copy(clean_ref.at[which], keyval.at[OWN, which], local_sem.at[3 + which])

    def above_copy(h, which):
        return remote(
            clean_ref.at[which, :, lanes(h)], keyval.at[ABOVE, which, :, lanes(h)],
            clean_send.at[0, h, which], clean_recv.at[0, h, which], below, head,
        )

    def across_copy(h, which, relay):
        src = keyval.at[ABOVE] if relay else clean_ref
        return remote(
            src.at[which, :, lanes(h)], keyval.at[ACROSS, which, :, lanes(h)],
            clean_send.at[1, h, which], clean_recv.at[1, h, which], far, head,
        )

    def query_copy(h):
        return remote(
            query.at[MINE, :, lanes(h)], query.at[PARTNER, :, lanes(h)],
            query_send.at[h], query_recv.at[h], near, head,
        )

    def part_copy(h):
        return remote(part.at[h], got.at[h], part_send.at[h, 0], part_recv.at[h, 0], near, head)

    def stat_copy(h):
        return remote(part_stat.at[h], got_stat.at[h], part_send.at[h, 1], part_recv.at[h, 1], near, head)

    def out_columns(h):
        return pl.ds(pl.multiple_of((head * heads_here + h) * HEAD_DIM, HEAD_DIM), HEAD_DIM)

    def out_copy(h, k):
        to = peers[k]
        return remote(
            final.at[h, pl.ds(pl.multiple_of(to * rows, rows), rows), :], out_ref.at[:, out_columns(h)],
            out_send.at[h, k], out_recv.at[h, k], group, to,
        )

    def out_local(h):
        return pltpu.make_async_copy(final.at[h, my_rows, :], out_ref.at[:, out_columns(h)], local_sem.at[5 + h])

    barrier = pltpu.get_barrier_semaphore()
    for to in peers:
        pl.semaphore_signal(barrier, inc=1, device_id=(group, to), device_id_type=MESH)
    for to in (near, far, below, above):
        pl.semaphore_signal(barrier, inc=1, device_id=(to, head), device_id_type=MESH)
    pl.semaphore_wait(barrier, len(peers) + 4)

    others = range(len(peers))
    both = range(2)
    for k in others:
        noisy_copy(0, k).start()
    noisy_local(0).start()
    for h in range(heads_here):
        for which in both:
            above_copy(h, which).start()

            @pl.when(column < 2)
            def _():
                across_copy(h, which, False).start()

    for which in (1, 2):
        noisy_local(which).start()
        own_copy(which - 1).start()
    accum[...] = jnp.zeros_like(accum)
    total[...] = jnp.zeros_like(total)
    peak[...] = jnp.full_like(peak, -FAR)

    noisy_local(0).wait()
    for k in others:
        noisy_copy(0, k).wait_recv()
    for h in range(heads_here):
        query_copy(h).start()
    for which in (1, 2):
        for k in others:
            noisy_copy(which, k).start()

    def attend(slot, whose, h, keep):
        lane = pl.ds(pl.multiple_of(h * HEAD_DIM, HEAD_DIM), HEAD_DIM)
        scores = lax.dot_general(
            keyval[slot, 0, :, lane], query[whose, :, lane], (((1,), (1,)), ((), ())),
            preferred_element_type=jnp.float32,
        )
        before = peak[whose, h]
        largest = jnp.where(keep, jnp.max(scores, axis=0, keepdims=True), -FAR)
        now = jnp.maximum(before, largest)
        expo = jnp.exp2((scores - jnp.where(keep, now, FAR)) * EXP2_SCALE)
        factor = jnp.exp2((before - now) * EXP2_SCALE)
        added = lax.dot_general(
            keyval[slot, 1, :, lane], expo.astype(jnp.bfloat16), (((0,), (0,)), ((), ())),
            preferred_element_type=jnp.float32,
        )
        peak[whose, h] = now
        total[whose, h] = total[whose, h] * factor + jnp.sum(expo, axis=0, keepdims=True)
        accum[whose, h] = accum[whose, h] * factor + added

    def merge(h):
        part_copy(h).wait_recv()
        stat_copy(h).wait_recv()
        here, there = peak[MINE, h], got_stat[h, 0:1, :]
        now = jnp.maximum(here, there)
        a = jnp.exp2((here - now) * EXP2_SCALE)
        b = jnp.exp2((there - now) * EXP2_SCALE)
        inverse = 1.0 / (total[MINE, h] * a + got_stat[h, 1:2, :] * b)
        summed = accum[MINE, h] * (a * inverse) + got[h].astype(jnp.float32) * (b * inverse)
        final[h] = jnp.transpose(summed).astype(final.dtype)
        for k in others:
            out_copy(h, k).start()
        out_local(h).start()

    def hand_over(h):
        part[h] = accum[PARTNER, h].astype(part.dtype)
        part_stat[h, 0:1, :] = peak[PARTNER, h]
        part_stat[h, 1:2, :] = total[PARTNER, h]
        part_copy(h).start()
        stat_copy(h).start()

    def take_above(h):
        for which in both:
            above_copy(h, which).wait_recv()

            @pl.when(column >= 2)
            def _():
                across_copy(h, which, True).start()

    def take_across(h):
        for which in both:
            across_copy(h, which, False).wait_recv()

    def take_noisy():
        for which in (1, 2):
            noisy_local(which).wait()
            for k in others:
                noisy_copy(which, k).wait_recv()

    def take_own():
        for which in both:
            own_copy(which).wait()

    hooks = {}
    seen = set()
    for i, (slot, whose, h) in enumerate(STEPS):
        todo = hooks.setdefault(i, [])
        if whose == PARTNER and ("query", h) not in seen:
            seen.add(("query", h))
            todo.append(functools.partial(lambda h: query_copy(h).wait_recv(), h))
        if slot is None and "own" not in seen:
            seen.add("own")
            todo.append(take_own)
        if slot == ABOVE:
            todo.append(functools.partial(take_above, h))
        if slot == ACROSS and ("across", h) not in seen:
            seen.add(("across", h))
            todo.append(functools.partial(take_across, h))
        if slot == NOISY and "noisy" not in seen:
            seen.add("noisy")
            todo.append(take_noisy)
    after = {}
    for h in range(heads_here):
        last = max(i for i, (_, whose, of) in enumerate(STEPS) if whose == PARTNER and of == h)
        after.setdefault(last, []).append(functools.partial(hand_over, h))
    merge_after = {10: 0, 13: 1, 14: 2}
    for i, h in merge_after.items():
        after.setdefault(i, []).append(functools.partial(merge, h))

    def distance(slot, whose, is_odd):
        if slot == NOISY:
            return -1
        if whose == MINE:
            return 3 if slot == ABOVE else (2 if is_odd else 0)
        return 1 if slot == ACROSS else (2 if is_odd else 0)

    def one(step, carry):
        for i, todo in hooks.items():
            if todo:

                @pl.when(step == i)
                def _():
                    for act in todo:
                        act()

        shared = jnp.where(odd == 1, ABOVE, OWN)
        slot = lookup(step, [-1 if s is None else s for s, _, _ in STEPS])
        slot = jnp.where(slot < 0, shared, slot)
        whose = lookup(step, [w for _, w, _ in STEPS])
        h = lookup(step, [h for _, _, h in STEPS])
        at = jnp.where(
            odd == 1,
            lookup(step, [distance(s, w, True) for s, w, _ in STEPS]),
            lookup(step, [distance(s, w, False) for s, w, _ in STEPS]),
        )
        keep = at < 0
        for j in range(REACH):
            keep = keep | ((at == j) & jnp.where(whose == MINE, mine_ok[j], near_ok[j]))
        attend(slot, whose, h, keep)
        for i, todo in after.items():

            @pl.when(step == i)
            def _():
                for act in todo:
                    act()

        return carry

    lax.fori_loop(0, len(STEPS), one, 0)

    for h in range(heads_here):
        out_local(h).wait()
        query_copy(h).wait_send()
        part_copy(h).wait_send()
        stat_copy(h).wait_send()
        for which in both:
            above_copy(h, which).wait_send()
            across_copy(h, which, False).wait_send()
        for k in others:
            out_copy(h, k).wait()
            noisy_copy(h, k).wait_send()


def on_device(groups, heads_axis, noisy_qkv, clean_kv, video_lengths, pattern):
    noisy = jnp.transpose(noisy_qkv, (1, 0, 2))
    clean = jnp.transpose(clean_kv, (1, 0, 2))
    _, tokens, width = clean.shape
    heads_here = width // HEAD_DIM
    rows, features = noisy.shape[1:]
    dma = pltpu.SemaphoreType.DMA
    peers = heads_axis - 1
    flops = 2 * 2 * tokens * tokens * width * (REACH + 1)
    return pl.pallas_call(
        functools.partial(kernel, groups, heads_axis),
        out_shape=jax.ShapeDtypeStruct((rows, features), noisy.dtype),
        in_specs=[pl.BlockSpec(memory_space=pl.ANY)] * 2 + [pl.BlockSpec(memory_space=pltpu.SMEM)] * 2,
        out_specs=pl.BlockSpec(memory_space=pl.ANY),
        scratch_shapes=[
            pltpu.VMEM((2, tokens, width), noisy.dtype),
            pltpu.VMEM((4, 2, tokens, width), noisy.dtype),
            pltpu.VMEM((2, heads_here, HEAD_DIM, tokens), jnp.float32),
            pltpu.VMEM((2, heads_here, 1, tokens), jnp.float32),
            pltpu.VMEM((2, heads_here, 1, tokens), jnp.float32),
            pltpu.VMEM((heads_here, HEAD_DIM, tokens), noisy.dtype),
            pltpu.VMEM((heads_here, 2, tokens), jnp.float32),
            pltpu.VMEM((heads_here, HEAD_DIM, tokens), noisy.dtype),
            pltpu.VMEM((heads_here, 2, tokens), jnp.float32),
            pltpu.VMEM((heads_here, tokens, HEAD_DIM), noisy.dtype),
            dma((3, peers)), dma((3, peers)),
            dma((2, heads_here, 2)), dma((2, heads_here, 2)),
            dma((heads_here,)), dma((heads_here,)),
            dma((heads_here, 2)), dma((heads_here, 2)),
            dma((heads_here, peers)), dma((heads_here, peers)),
            dma((5 + heads_here,)),
        ],
        compiler_params=pltpu.CompilerParams(
            collective_id=0, has_side_effects=True, vmem_limit_bytes=56 * 2**20
        ),
        cost_estimate=pl.CostEstimate(
            flops=flops, bytes_accessed=8 * tokens * width, transcendentals=tokens * tokens * heads_here * (REACH + 1)
        ),
    )(noisy, clean, video_lengths, pattern)


def solution(mesh):
    groups, heads_axis = mesh.shape["group"], mesh.shape["head"]
    return jax.shard_map(
        functools.partial(on_device, groups, heads_axis),
        mesh=mesh,
        in_specs=(P(("group", "head"), None, None), P("group", None, "head"), P(), P()),
        out_specs=P(("group", "head"), None),
        check_vma=False,
    )
```

time: 242 us -> 86.3 us (0.36)
  the two profiles are of different devices: /device:TPU:128 before, /device:TPU:1 now
where the time goes in v1:
time: 86.3 us; the launch traced here: 86.1 us
  Pallas kernels  81.2 us (94%)
  local copies, waits for them, and re-layouts  4.82 us (6%)
    pallas_call x1, Pallas kernels, on_device(): pl.pallas_call(functools.partial(kernel, groups, heads_axis), out_shape=j...  81.2 us
    unnamed x2, local copies, waits for them, and re-layouts  4.82 us

profile of v1, /device:TPU:1, one launch (start us, length us, event | category | flops | bytes accessed | tf_op | source)
XLA Modules:
  0.0 86.1 jit_solution(6061542067929597295)
XLA Ops:
  0.0 2.8 %copy.7 = bf16[1024,2,384]{2,0,1:T(8,128)(2,1)} copy(bf16[1024,2,384]{2,1,0:T(2,128)(2,1)} %param.5) | data formatting | bytes 3145728 | tf_op args[1]
  2.8 81.2 %shard_map.46 = bf16[128,3072]{1,0:T(8,128)(2,1)} custom-call(bf16[3,128,3072]{2,1,0:T(8,128)(2,1)} %bitcast.5, bf16[2,1024,384]{2,1,0:T(8,128)(2,1)} %bitcast.4, s32[4]{0:T(128)} %lengths_ref.1, s32[4,4]{1,0:T(4,128)} %pattern_ref.1), custom_call_target="tpu_custom_call" | custom-call | flops 8053063680 | bytes 3145728 | tf_op jit(solution)/shard_map/pallas_call | solution.py:342
  84.0 2.1 %copy.9 = bf16[128,3072]{1,0:T(8,128)(2,1)} copy(bf16[128,3072]{1,0:T(8,128)(2,1)} %shard_map.46) | data formatting | bytes 1572864

commit v2 on v1

--- a/solution.py
+++ b/solution.py
@@ -17,23 +17,27 @@
 NOISY, OWN, ABOVE, ACROSS = 0, 1, 2, 3
 MINE, PARTNER = 0, 1
 
+SPLIT = 2
+TILES = 2
+
 STEPS = (
     (ABOVE, MINE, 0),
     (ACROSS, MINE, 0),
     (None, PARTNER, 0),
     (ACROSS, PARTNER, 0),
+    (ABOVE, MINE, 1),
+    (None, PARTNER, 1),
     (NOISY, MINE, 0),
-    (ABOVE, MINE, 1),
-    (NOISY, MINE, 1),
-    (None, PARTNER, 1),
     (ACROSS, PARTNER, 1),
     (ACROSS, MINE, 1),
+    (NOISY, MINE, 1),
+    (NOISY, MINE, 2),
     (ABOVE, MINE, 2),
-    (NOISY, MINE, 2),
     (None, PARTNER, 2),
-    (ACROSS, PARTNER, 2),
-    (ACROSS, MINE, 2),
 )
+PASS_ON = {0: (2, 3), 1: (4,), 3: (5,), 4: (6, 7), 6: (8,), 8: (9,), 9: (10,), 11: (11,)}
+HAND_OVER_AFTER = {3: 0, 7: 1}
+MERGE_AFTER = {10: 0}
 
 
 def lookup(step, values):
@@ -114,18 +118,24 @@
     def own_copy(which):
         return pltpu.make_async_copy(clean_ref.at[which], keyval.at[OWN, which], local_sem.at[3 + which])
 
-    def above_copy(h, which):
+    def piece(i):
+        h, rest = divmod(i, 2 * SPLIT)
+        which, part_of = divmod(rest, SPLIT)
+        n = keyval.shape[2] // SPLIT
+        return which, pl.ds(part_of * n, n), lanes(h)
+
+    pieces = range(heads_here * 2 * SPLIT)
+
+    def above_copy(i):
+        at = piece(i)
         return remote(
-            clean_ref.at[which, :, lanes(h)], keyval.at[ABOVE, which, :, lanes(h)],
-            clean_send.at[0, h, which], clean_recv.at[0, h, which], below, head,
-        )
-
-    def across_copy(h, which, relay):
-        src = keyval.at[ABOVE] if relay else clean_ref
-        return remote(
-            src.at[which, :, lanes(h)], keyval.at[ACROSS, which, :, lanes(h)],
-            clean_send.at[1, h, which], clean_recv.at[1, h, which], far, head,
-        )
+            clean_ref.at[at], keyval.at[(ABOVE, *at)], clean_send.at[0, i], clean_recv.at[0, i], below, head
+        )
+
+    def across_copy(i, relay):
+        at = piece(i)
+        src = keyval.at[(ABOVE, *at)] if relay else clean_ref.at[at]
+        return remote(src, keyval.at[(ACROSS, *at)], clean_send.at[1, i], clean_recv.at[1, i], far, head)
 
     def query_copy(h):
         return remote(
@@ -133,17 +143,23 @@
             query_send.at[h], query_recv.at[h], near, head,
         )
 
-    def part_copy(h):
-        return remote(part.at[h], got.at[h], part_send.at[h, 0], part_recv.at[h, 0], near, head)
-
-    def stat_copy(h):
-        return remote(part_stat.at[h], got_stat.at[h], part_send.at[h, 1], part_recv.at[h, 1], near, head)
+    tokens = query.shape[1]
+
+    def part_copies(h, tile=None):
+        at = pl.ds(0, tokens) if tile is None else pl.ds(tile * (tokens // TILES), tokens // TILES)
+        sem = h if tile is None else h + tile
+        return (
+            remote(part.at[h, :, at], got.at[h, :, at], part_send.at[sem, 0], part_recv.at[sem, 0], near, head),
+            remote(
+                part_stat.at[h, :, at], got_stat.at[h, :, at], part_send.at[sem, 1], part_recv.at[sem, 1], near, head
+            ),
+        )
 
     def out_columns(h):
         return pl.ds(pl.multiple_of((head * heads_here + h) * HEAD_DIM, HEAD_DIM), HEAD_DIM)
 
-    def out_copy(h, k):
-        to = peers[k]
+    def out_copy(h, to):
+        k = lax.rem(to - head + heads_axis, heads_axis)
         return remote(
             final.at[h, pl.ds(pl.multiple_of(to * rows, rows), rows), :], out_ref.at[:, out_columns(h)],
             out_send.at[h, k], out_recv.at[h, k], group, to,
@@ -160,17 +176,16 @@
     pl.semaphore_wait(barrier, len(peers) + 4)
 
     others = range(len(peers))
-    both = range(2)
     for k in others:
         noisy_copy(0, k).start()
     noisy_local(0).start()
-    for h in range(heads_here):
-        for which in both:
-            above_copy(h, which).start()
-
-            @pl.when(column < 2)
-            def _():
-                across_copy(h, which, False).start()
+    for i in pieces:
+        above_copy(i).start()
+
+    @pl.when(column < 2)
+    def _():
+        for i in pieces:
+            across_copy(i, False).start()
 
     for which in (1, 2):
         noisy_local(which).start()
@@ -179,6 +194,15 @@
     total[...] = jnp.zeros_like(total)
     peak[...] = jnp.full_like(peak, -FAR)
 
+    def pass_on(i):
+        above_copy(i).wait_recv()
+
+        @pl.when(column >= 2)
+        def _():
+            across_copy(i, True).start()
+
+    for i in range(PASS_ON[0][0]):
+        pass_on(i)
     noisy_local(0).wait()
     for k in others:
         noisy_copy(0, k).wait_recv()
@@ -188,13 +212,13 @@
         for k in others:
             noisy_copy(which, k).start()
 
-    def attend(slot, whose, h, keep):
+    def attend(slot, whose, h, keep, at):
         lane = pl.ds(pl.multiple_of(h * HEAD_DIM, HEAD_DIM), HEAD_DIM)
         scores = lax.dot_general(
-            keyval[slot, 0, :, lane], query[whose, :, lane], (((1,), (1,)), ((), ())),
+            keyval[slot, 0, :, lane], query[whose, at, lane], (((1,), (1,)), ((), ())),
             preferred_element_type=jnp.float32,
         )
-        before = peak[whose, h]
+        before = peak[whose, h, :, at]
         largest = jnp.where(keep, jnp.max(scores, axis=0, keepdims=True), -FAR)
         now = jnp.maximum(before, largest)
         expo = jnp.exp2((scores - jnp.where(keep, now, FAR)) * EXP2_SCALE)
@@ -203,42 +227,48 @@
             keyval[slot, 1, :, lane], expo.astype(jnp.bfloat16), (((0,), (0,)), ((), ())),
             preferred_element_type=jnp.float32,
         )
-        peak[whose, h] = now
-        total[whose, h] = total[whose, h] * factor + jnp.sum(expo, axis=0, keepdims=True)
-        accum[whose, h] = accum[whose, h] * factor + added
-
-    def merge(h):
-        part_copy(h).wait_recv()
-        stat_copy(h).wait_recv()
-        here, there = peak[MINE, h], got_stat[h, 0:1, :]
+        peak[whose, h, :, at] = now
+        total[whose, h, :, at] = total[whose, h, :, at] * factor + jnp.sum(expo, axis=0, keepdims=True)
+        accum[whose, h, :, at] = accum[whose, h, :, at] * factor + added
+
+    every = pl.ds(0, tokens)
+
+    def tile_of(t):
+        return pl.ds(t * (tokens // TILES), tokens // TILES)
+
+    def merge(h, tile=None):
+        at = every if tile is None else tile_of(tile)
+        for copy in part_copies(h, tile):
+            copy.wait_recv()
+        here, there = peak[MINE, h, :, at], got_stat[h, 0:1, at]
         now = jnp.maximum(here, there)
         a = jnp.exp2((here - now) * EXP2_SCALE)
         b = jnp.exp2((there - now) * EXP2_SCALE)
-        inverse = 1.0 / (total[MINE, h] * a + got_stat[h, 1:2, :] * b)
-        summed = accum[MINE, h] * (a * inverse) + got[h].astype(jnp.float32) * (b * inverse)
-        final[h] = jnp.transpose(summed).astype(final.dtype)
-        for k in others:
-            out_copy(h, k).start()
-        out_local(h).start()
-
-    def hand_over(h):
-        part[h] = accum[PARTNER, h].astype(part.dtype)
-        part_stat[h, 0:1, :] = peak[PARTNER, h]
-        part_stat[h, 1:2, :] = total[PARTNER, h]
-        part_copy(h).start()
-        stat_copy(h).start()
-
-    def take_above(h):
-        for which in both:
-            above_copy(h, which).wait_recv()
-
-            @pl.when(column >= 2)
+        inverse = 1.0 / (total[MINE, h, :, at] * a + got_stat[h, 1:2, at] * b)
+        summed = accum[MINE, h, :, at] * (a * inverse) + got[h, :, at].astype(jnp.float32) * (b * inverse)
+        final[h, at, :] = jnp.transpose(summed).astype(final.dtype)
+        for j in range(at.start // rows, (at.start + at.size) // rows):
+
+            @pl.when(head != j)
             def _():
-                across_copy(h, which, True).start()
+                out_copy(h, j).start()
+
+            @pl.when(head == j)
+            def _():
+                out_local(h).start()
+
+    def hand_over(h, tile=None):
+        at = every if tile is None else tile_of(tile)
+        part[h, :, at] = accum[PARTNER, h, :, at].astype(part.dtype)
+        part_stat[h, 0:1, at] = peak[PARTNER, h, :, at]
+        part_stat[h, 1:2, at] = total[PARTNER, h, :, at]
+        for copy in part_copies(h, tile):
+            copy.start()
 
     def take_across(h):
-        for which in both:
-            across_copy(h, which, False).wait_recv()
+        for i in pieces:
+            if i // (2 * SPLIT) == h:
+                across_copy(i, False).wait_recv()
 
     def take_noisy():
         for which in (1, 2):
@@ -247,21 +277,21 @@
                 noisy_copy(which, k).wait_recv()
 
     def take_own():
-        for which in both:
+        for which in range(2):
             own_copy(which).wait()
 
     hooks = {}
     seen = set()
     for i, (slot, whose, h) in enumerate(STEPS):
         todo = hooks.setdefault(i, [])
+        for j in PASS_ON.get(i, ()):
+            todo.append(functools.partial(pass_on, j))
         if whose == PARTNER and ("query", h) not in seen:
             seen.add(("query", h))
             todo.append(functools.partial(lambda h: query_copy(h).wait_recv(), h))
         if slot is None and "own" not in seen:
             seen.add("own")
             todo.append(take_own)
-        if slot == ABOVE:
-            todo.append(functools.partial(take_above, h))
         if slot == ACROSS and ("across", h) not in seen:
             seen.add(("across", h))
             todo.append(functools.partial(take_across, h))
@@ -269,11 +299,9 @@
             seen.add("noisy")
             todo.append(take_noisy)
     after = {}
-    for h in range(heads_here):
-        last = max(i for i, (_, whose, of) in enumerate(STEPS) if whose == PARTNER and of == h)
-        after.setdefault(last, []).append(functools.partial(hand_over, h))
-    merge_after = {10: 0, 13: 1, 14: 2}
-    for i, h in merge_after.items():
+    for i, h in HAND_OVER_AFTER.items():
+        after.setdefault(i, []).append(functools.partial(hand_over, h))
+    for i, h in MERGE_AFTER.items():
         after.setdefault(i, []).append(functools.partial(merge, h))
 
     def distance(slot, whose, is_odd):
@@ -305,7 +333,7 @@
         keep = at < 0
         for j in range(REACH):
             keep = keep | ((at == j) & jnp.where(whose == MINE, mine_ok[j], near_ok[j]))
-        attend(slot, whose, h, keep)
+        attend(slot, whose, h, keep, every)
         for i, todo in after.items():
 
             @pl.when(step == i)
@@ -317,17 +345,27 @@
 
     lax.fori_loop(0, len(STEPS), one, 0)
 
+    last = heads_here - 1
+    take_across(last)
+    for tile in range(TILES):
+        attend(ACROSS, PARTNER, last, near_ok[1], tile_of(tile))
+        hand_over(last, tile)
+    merge(1)
+    attend(ACROSS, MINE, last, (mine_ok[0] & (odd == 0)) | (mine_ok[2] & (odd == 1)), every)
+    for tile in range(TILES):
+        merge(last, tile)
+
     for h in range(heads_here):
         out_local(h).wait()
         query_copy(h).wait_send()
-        part_copy(h).wait_send()
-        stat_copy(h).wait_send()
-        for which in both:
-            above_copy(h, which).wait_send()
-            across_copy(h, which, False).wait_send()
+        for copy in [c for t in range(TILES) for c in part_copies(h, t)] if h == last else part_copies(h):
+            copy.wait_send()
         for k in others:
-            out_copy(h, k).wait()
+            out_copy(h, peers[k]).wait()
             noisy_copy(h, k).wait_send()
+    for i in pieces:
+        above_copy(i).wait_send()
+        across_copy(i, False).wait_send()
 
 
 def on_device(groups, heads_axis, noisy_qkv, clean_kv, video_lengths, pattern):
@@ -356,10 +394,10 @@
             pltpu.VMEM((heads_here, 2, tokens), jnp.float32),
             pltpu.VMEM((heads_here, tokens, HEAD_DIM), noisy.dtype),
             dma((3, peers)), dma((3, peers)),
-            dma((2, heads_here, 2)), dma((2, heads_here, 2)),
+            dma((2, heads_here * 2 * SPLIT)), dma((2, heads_here * 2 * SPLIT)),
             dma((heads_here,)), dma((heads_here,)),
-            dma((heads_here, 2)), dma((heads_here, 2)),
-            dma((heads_here, peers)), dma((heads_here, peers)),
+            dma((heads_here - 1 + TILES, 2)), dma((heads_here - 1 + TILES, 2)),
+            dma((heads_here, heads_axis)), dma((heads_here, heads_axis)),
             dma((5 + heads_here,)),
         ],
         compiler_params=pltpu.CompilerParams(

time: 86.3 us -> 72.3 us (0.84)
  Pallas kernels: 81.2 us -> 67.3 us
    pallas_call x1, Pallas kernels: 81.2 us -> 67.3 us  [on_device(): pl.pallas_call(functools.partial(kernel, groups, heads_axis), out_shape=j...]
where the time goes in v2:
time: 72.3 us; the launch traced here: 72.2 us
  Pallas kernels  67.3 us (93%)
  local copies, waits for them, and re-layouts  4.82 us (7%)
    pallas_call x1, Pallas kernels, on_device(): pl.pallas_call(functools.partial(kernel, groups, heads_axis), out_shape=j...  67.3 us
    unnamed x2, local copies, waits for them, and re-layouts  4.82 us

profile of v2, /device:TPU:1, one launch (start us, length us, event | category | flops | bytes accessed | tf_op | source)
XLA Modules:
  0.0 72.2 jit_solution(1052807091221372683)
XLA Ops:
  0.0 2.8 %copy.7 = bf16[1024,2,384]{2,0,1:T(8,128)(2,1)} copy(bf16[1024,2,384]{2,1,0:T(2,128)(2,1)} %param.5) | data formatting | bytes 3145728 | tf_op args[1]
  2.8 67.3 %shard_map.46 = bf16[128,3072]{1,0:T(8,128)(2,1)} custom-call(bf16[3,128,3072]{2,1,0:T(8,128)(2,1)} %bitcast.5, bf16[2,1024,384]{2,1,0:T(8,128)(2,1)} %bitcast.4, s32[4]{0:T(128)} %lengths_ref.1, s32[4,4]{1,0:T(4,128)} %pattern_ref.1), custom_call_target="tpu_custom_call" | custom-call | flops 8053063680 | bytes 3145728 | tf_op jit(solution)/shard_map/pallas_call | solution.py:380
  70.1 2.1 %copy.9 = bf16[128,3072]{1,0:T(8,128)(2,1)} copy(bf16[128,3072]{1,0:T(8,128)(2,1)} %shard_map.46) | data formatting | bytes 1572864

commit v3 on v2

--- a/solution.py
+++ b/solution.py
@@ -67,13 +67,13 @@
 def kernel(
     groups, heads_axis,
     noisy_ref, clean_ref, lengths_ref, pattern_ref, out_ref,
-    query, keyval, accum, peak, total, part, part_stat, got, got_stat, final,
+    paired, query, keyval, accum, peak, total, part, part_stat, got, got_stat, final,
     noisy_send, noisy_recv, clean_send, clean_recv, query_send, query_recv,
     part_send, part_recv, out_send, out_recv, local_sem,
 ):
     group, head = lax.axis_index("group"), lax.axis_index("head")
     rows = noisy_ref.shape[1]
-    width = keyval.shape[3]
+    tokens, width = query.shape[1:]
     heads_here = width // HEAD_DIM
     column = lax.rem(group, ROW)
     odd = lax.rem(column, 2)
@@ -115,8 +115,20 @@
             noisy_ref.at[which, :, columns(head)], noisy_target(which).at[my_rows, :], local_sem.at[which]
         )
 
-    def own_copy(which):
-        return pltpu.make_async_copy(clean_ref.at[which], keyval.at[OWN, which], local_sem.at[3 + which])
+    def paired_copy(h):
+        return pltpu.make_async_copy(clean_ref.at[:, h], paired.at[h], local_sem.at[3 + h])
+
+    def part_pairs(h):
+        n = 2 * HEAD_DIM
+        rows_of = paired.at[h].reshape(2 * tokens, HEAD_DIM)
+        to, source = (lax.broadcasted_iota(jnp.int32, (n, n), axis) for axis in (0, 1))
+        pick = source == 2 * lax.rem(to, HEAD_DIM) + to // HEAD_DIM
+        pick = jnp.where(pick, 1.0, 0.0).astype(keyval.dtype)
+        for i in range(2 * tokens // n):
+            moved = jnp.dot(pick, rows_of[pl.ds(i * n, n), :], preferred_element_type=jnp.float32)
+            moved = moved.astype(keyval.dtype)
+            for which in range(2):
+                keyval[OWN, which, pl.ds(i * HEAD_DIM, HEAD_DIM), lanes(h)] = moved[which * HEAD_DIM:(which + 1) * HEAD_DIM]
 
     def piece(i):
         h, rest = divmod(i, 2 * SPLIT)
@@ -129,12 +141,12 @@
     def above_copy(i):
         at = piece(i)
         return remote(
-            clean_ref.at[at], keyval.at[(ABOVE, *at)], clean_send.at[0, i], clean_recv.at[0, i], below, head
+            keyval.at[(OWN, *at)], keyval.at[(ABOVE, *at)], clean_send.at[0, i], clean_recv.at[0, i], below, head
         )
 
     def across_copy(i, relay):
         at = piece(i)
-        src = keyval.at[(ABOVE, *at)] if relay else clean_ref.at[at]
+        src = keyval.at[(ABOVE if relay else OWN, *at)]
         return remote(src, keyval.at[(ACROSS, *at)], clean_send.at[1, i], clean_recv.at[1, i], far, head)
 
     def query_copy(h):
@@ -142,8 +154,6 @@
             query.at[MINE, :, lanes(h)], query.at[PARTNER, :, lanes(h)],
             query_send.at[h], query_recv.at[h], near, head,
         )
-
-    tokens = query.shape[1]
 
     def part_copies(h, tile=None):
         at = pl.ds(0, tokens) if tile is None else pl.ds(tile * (tokens // TILES), tokens // TILES)
@@ -166,30 +176,33 @@
         )
 
     def out_local(h):
-        return pltpu.make_async_copy(final.at[h, my_rows, :], out_ref.at[:, out_columns(h)], local_sem.at[5 + h])
+        return pltpu.make_async_copy(final.at[h, my_rows, :], out_ref.at[:, out_columns(h)], local_sem.at[3 + heads_here + h])
 
     barrier = pltpu.get_barrier_semaphore()
     for to in peers:
         pl.semaphore_signal(barrier, inc=1, device_id=(group, to), device_id_type=MESH)
     for to in (near, far, below, above):
         pl.semaphore_signal(barrier, inc=1, device_id=(to, head), device_id_type=MESH)
-    pl.semaphore_wait(barrier, len(peers) + 4)
-
+    for h in range(heads_here):
+        paired_copy(h).start()
+    for which in range(3):
+        noisy_local(which).start()
     others = range(len(peers))
-    for k in others:
-        noisy_copy(0, k).start()
-    noisy_local(0).start()
-    for i in pieces:
-        above_copy(i).start()
-
-    @pl.when(column < 2)
-    def _():
+    for h in range(heads_here):
+        paired_copy(h).wait()
+        part_pairs(h)
+        if h == 0:
+            pl.semaphore_wait(barrier, len(peers) + 4)
+            for k in others:
+                noisy_copy(0, k).start()
         for i in pieces:
-            across_copy(i, False).start()
-
-    for which in (1, 2):
-        noisy_local(which).start()
-        own_copy(which - 1).start()
+            if i // (2 * SPLIT) == h:
+                above_copy(i).start()
+
+                @pl.when(column < 2)
+                def _():
+                    across_copy(i, False).start()
+
     accum[...] = jnp.zeros_like(accum)
     total[...] = jnp.zeros_like(total)
     peak[...] = jnp.full_like(peak, -FAR)
@@ -276,10 +289,6 @@
             for k in others:
                 noisy_copy(which, k).wait_recv()
 
-    def take_own():
-        for which in range(2):
-            own_copy(which).wait()
-
     hooks = {}
     seen = set()
     for i, (slot, whose, h) in enumerate(STEPS):
@@ -289,9 +298,6 @@
         if whose == PARTNER and ("query", h) not in seen:
             seen.add(("query", h))
             todo.append(functools.partial(lambda h: query_copy(h).wait_recv(), h))
-        if slot is None and "own" not in seen:
-            seen.add("own")
-            todo.append(take_own)
         if slot == ACROSS and ("across", h) not in seen:
             seen.add(("across", h))
             todo.append(functools.partial(take_across, h))
@@ -370,9 +376,9 @@
 
 def on_device(groups, heads_axis, noisy_qkv, clean_kv, video_lengths, pattern):
     noisy = jnp.transpose(noisy_qkv, (1, 0, 2))
-    clean = jnp.transpose(clean_kv, (1, 0, 2))
-    _, tokens, width = clean.shape
+    tokens, _, width = clean_kv.shape
     heads_here = width // HEAD_DIM
+    clean = jnp.transpose(clean_kv.reshape(tokens, 2, heads_here, HEAD_DIM), (0, 2, 1, 3))
     rows, features = noisy.shape[1:]
     dma = pltpu.SemaphoreType.DMA
     peers = heads_axis - 1
@@ -383,6 +389,7 @@
         in_specs=[pl.BlockSpec(memory_space=pl.ANY)] * 2 + [pl.BlockSpec(memory_space=pltpu.SMEM)] * 2,
         out_specs=pl.BlockSpec(memory_space=pl.ANY),
         scratch_shapes=[
+            pltpu.VMEM((heads_here, tokens, 2, HEAD_DIM), noisy.dtype),
             pltpu.VMEM((2, tokens, width), noisy.dtype),
             pltpu.VMEM((4, 2, tokens, width), noisy.dtype),
             pltpu.VMEM((2, heads_here, HEAD_DIM, tokens), jnp.float32),
@@ -398,7 +405,7 @@
             dma((heads_here,)), dma((heads_here,)),
             dma((heads_here - 1 + TILES, 2)), dma((heads_here - 1 + TILES, 2)),
             dma((heads_here, heads_axis)), dma((heads_here, heads_axis)),
-            dma((5 + heads_here,)),
+            dma((3 + 2 * heads_here,)),
         ],
         compiler_params=pltpu.CompilerParams(
             collective_id=0, has_side_effects=True, vmem_limit_bytes=56 * 2**20

time: 72.3 us -> 69.9 us (0.967)
  local copies, waits for them, and re-layouts: 4.82 us -> 2.06 us
    unnamed x2 -> x1, local copies, waits for them, and re-layouts: 4.82 us -> 2.06 us
where the time goes in v3:
time: 69.9 us; the launch traced here: 69.7 us
  Pallas kernels  67.6 us (97%)
  local copies, waits for them, and re-layouts  2.06 us (3%)
    pallas_call x1, Pallas kernels, on_device(): pl.pallas_call(functools.partial(kernel, groups, heads_axis), out_shape=j...  67.6 us
    unnamed x1, local copies, waits for them, and re-layouts  2.06 us

profile of v3, /device:TPU:1, one launch (start us, length us, event | category | flops | bytes accessed | tf_op | source)
XLA Modules:
  0.0 69.7 jit_solution(3918304261278689794)
XLA Ops:
  0.0 67.6 %shard_map.46 = bf16[128,3072]{1,0:T(8,128)(2,1)} custom-call(bf16[3,128,3072]{2,1,0:T(8,128)(2,1)} %bitcast.4, bf16[1024,3,2,128]{3,2,1,0:T(2,128)(2,1)} %bitcast.5, s32[4]{0:T(128)} %lengths_ref.1, s32[4,4]{1,0:T(4,128)} %pattern_ref.1), custom_call_target="tpu_custom_call" | custom-call | flops 8053063680 | bytes 3145728 | tf_op jit(solution)/shard_map/pallas_call | solution.py:386
  67.6 2.1 %copy.6 = bf16[128,3072]{1,0:T(8,128)(2,1)} copy(bf16[128,3072]{1,0:T(8,128)(2,1)} %shard_map.46) | data formatting | bytes 1572864

commit v4 on v3

--- a/solution.py
+++ b/solution.py
@@ -18,7 +18,7 @@
 MINE, PARTNER = 0, 1
 
 SPLIT = 2
-TILES = 2
+TILES = 4
 
 STEPS = (
     (ABOVE, MINE, 0),
@@ -32,12 +32,12 @@
     (ACROSS, MINE, 1),
     (NOISY, MINE, 1),
     (NOISY, MINE, 2),
-    (ABOVE, MINE, 2),
     (None, PARTNER, 2),
+    (ACROSS, PARTNER, 2),
 )
-PASS_ON = {0: (2, 3), 1: (4,), 3: (5,), 4: (6, 7), 6: (8,), 8: (9,), 9: (10,), 11: (11,)}
+PASS_ON = {0: (2, 3), 1: (4,), 3: (5,), 4: (6, 7), 5: (8,), 7: (9,), 8: (10,), 11: (11,)}
 HAND_OVER_AFTER = {3: 0, 7: 1}
-MERGE_AFTER = {10: 0}
+MERGE_AFTER = {9: 0}
 
 
 def lookup(step, values):
@@ -67,7 +67,7 @@
 def kernel(
     groups, heads_axis,
     noisy_ref, clean_ref, lengths_ref, pattern_ref, out_ref,
-    paired, query, keyval, accum, peak, total, part, part_stat, got, got_stat, final,
+    paired, query, keyval, accum, peak, total, part, part_stat, got, got_stat, final, even_scores, odd_scores, weights,
     noisy_send, noisy_recv, clean_send, clean_recv, query_send, query_recv,
     part_send, part_recv, out_send, out_recv, local_sem,
 ):
@@ -225,24 +225,31 @@
         for k in others:
             noisy_copy(which, k).start()
 
-    def attend(slot, whose, h, keep, at):
-        lane = pl.ds(pl.multiple_of(h * HEAD_DIM, HEAD_DIM), HEAD_DIM)
-        scores = lax.dot_general(
-            keyval[slot, 0, :, lane], query[whose, at, lane], (((1,), (1,)), ((), ())),
+    def lane_of(h):
+        return pl.ds(pl.multiple_of(h * HEAD_DIM, HEAD_DIM), HEAD_DIM)
+
+    def score(slot, whose, h, at):
+        return lax.dot_general(
+            keyval[slot, 0, :, lane_of(h)], query[whose, at, lane_of(h)], (((1,), (1,)), ((), ())),
             preferred_element_type=jnp.float32,
         )
+
+    def weigh(slot, whose, h, keep, at, scores, largest):
         before = peak[whose, h, :, at]
-        largest = jnp.where(keep, jnp.max(scores, axis=0, keepdims=True), -FAR)
-        now = jnp.maximum(before, largest)
+        now = jnp.maximum(before, jnp.where(keep, largest, -FAR))
         expo = jnp.exp2((scores - jnp.where(keep, now, FAR)) * EXP2_SCALE)
         factor = jnp.exp2((before - now) * EXP2_SCALE)
         added = lax.dot_general(
-            keyval[slot, 1, :, lane], expo.astype(jnp.bfloat16), (((0,), (0,)), ((), ())),
+            keyval[slot, 1, :, lane_of(h)], expo.astype(jnp.bfloat16), (((0,), (0,)), ((), ())),
             preferred_element_type=jnp.float32,
         )
         peak[whose, h, :, at] = now
         total[whose, h, :, at] = total[whose, h, :, at] * factor + jnp.sum(expo, axis=0, keepdims=True)
         accum[whose, h, :, at] = accum[whose, h, :, at] * factor + added
+
+    def attend(slot, whose, h, keep, at):
+        scores = score(slot, whose, h, at)
+        weigh(slot, whose, h, keep, at, scores, jnp.max(scores, axis=0, keepdims=True))
 
     every = pl.ds(0, tokens)
 
@@ -278,9 +285,9 @@
         for copy in part_copies(h, tile):
             copy.start()
 
-    def take_across(h):
+    def take_across(h, which=None):
         for i in pieces:
-            if i // (2 * SPLIT) == h:
+            if i // (2 * SPLIT) == h and which in (None, i // SPLIT % 2):
                 across_copy(i, False).wait_recv()
 
     def take_noisy():
@@ -291,7 +298,7 @@
 
     hooks = {}
     seen = set()
-    for i, (slot, whose, h) in enumerate(STEPS):
+    for i, (slot, whose, h) in enumerate(STEPS[:-1]):
         todo = hooks.setdefault(i, [])
         for j in PASS_ON.get(i, ()):
             todo.append(functools.partial(pass_on, j))
@@ -317,20 +324,22 @@
             return 3 if slot == ABOVE else (2 if is_odd else 0)
         return 1 if slot == ACROSS else (2 if is_odd else 0)
 
-    def one(step, carry):
-        for i, todo in hooks.items():
-            if todo:
+    def run(actions, step, parity):
+        for i, todo in actions.items():
+            if todo and i % 2 == parity:
 
                 @pl.when(step == i)
                 def _():
                     for act in todo:
                         act()
 
+    def operands(step):
         shared = jnp.where(odd == 1, ABOVE, OWN)
         slot = lookup(step, [-1 if s is None else s for s, _, _ in STEPS])
         slot = jnp.where(slot < 0, shared, slot)
-        whose = lookup(step, [w for _, w, _ in STEPS])
-        h = lookup(step, [h for _, _, h in STEPS])
+        return slot, lookup(step, [w for _, w, _ in STEPS]), lookup(step, [h for _, _, h in STEPS])
+
+    def kept(step, whose):
         at = jnp.where(
             odd == 1,
             lookup(step, [distance(s, w, True) for s, w, _ in STEPS]),
@@ -339,25 +348,70 @@
         keep = at < 0
         for j in range(REACH):
             keep = keep | ((at == j) & jnp.where(whose == MINE, mine_ok[j], near_ok[j]))
-        attend(slot, whose, h, keep, every)
-        for i, todo in after.items():
-
-            @pl.when(step == i)
-            def _():
-                for act in todo:
-                    act()
-
-        return carry
-
-    lax.fori_loop(0, len(STEPS), one, 0)
+        return keep
+
+    def begin(step, held):
+        return begin_at(*operands(step), held)
+
+    def begin_at(slot, whose, h, held):
+        scores = score(slot, whose, h, every)
+        held[...] = scores
+        return jnp.max(scores, axis=0, keepdims=True)
+
+    def finish(step, held, largest):
+        slot, whose, h = operands(step)
+        weigh(slot, whose, h, kept(step, whose), every, held[...], largest)
+
+    def two(pair, largest):
+        step = 2 * pair
+        run(hooks, step + 1, 1)
+        following = begin(step + 1, odd_scores)
+        finish(step, even_scores, largest)
+        run(after, step, 0)
+        run(hooks, step + 2, 0)
+        largest = begin(step + 2, even_scores)
+        finish(step + 1, odd_scores, following)
+        run(after, step + 1, 1)
+        return largest
+
+    for act in hooks.pop(0):
+        act()
+    largest = begin(0, even_scores)
+    final_steps = len(STEPS) - 2
+    largest = lax.fori_loop(0, final_steps // 2, two, largest)
 
     last = heads_here - 1
-    take_across(last)
+    for act in hooks.pop(final_steps):
+        act()
+    following = begin(final_steps, odd_scores)
+    finish(final_steps - 1, even_scores, largest)
+    take_across(last, 0)
+    largest = begin(final_steps + 1, even_scores)
+    finish(final_steps, odd_scores, following)
+
+    before = peak[PARTNER, last]
+    now = jnp.maximum(before, jnp.where(near_ok[1], largest, -FAR))
+    expo = jnp.exp2((even_scores[...] - jnp.where(near_ok[1], now, FAR)) * EXP2_SCALE)
+    factor = jnp.exp2((before - now) * EXP2_SCALE)
+    weights[...] = expo.astype(weights.dtype)
+    peak[PARTNER, last] = now
+    total[PARTNER, last] = total[PARTNER, last] * factor + jnp.sum(expo, axis=0, keepdims=True)
+    following = begin_at(ABOVE, MINE, last, odd_scores)
+    take_across(last, 1)
     for tile in range(TILES):
-        attend(ACROSS, PARTNER, last, near_ok[1], tile_of(tile))
+        at = tile_of(tile)
+        added = lax.dot_general(
+            keyval[ACROSS, 1, :, lanes(last)], weights[:, at], (((0,), (0,)), ((), ())),
+            preferred_element_type=jnp.float32,
+        )
+        n = tokens // TILES
+        accum[PARTNER, last, :, at] = accum[PARTNER, last, :, at] * factor[:, tile * n:(tile + 1) * n] + added
         hand_over(last, tile)
+    largest = begin_at(ACROSS, MINE, last, even_scores)
+    weigh(ABOVE, MINE, last, mine_ok[3], every, odd_scores[...], following)
     merge(1)
-    attend(ACROSS, MINE, last, (mine_ok[0] & (odd == 0)) | (mine_ok[2] & (odd == 1)), every)
+    keep = (mine_ok[0] & (odd == 0)) | (mine_ok[2] & (odd == 1))
+    weigh(ACROSS, MINE, last, keep, every, even_scores[...], largest)
     for tile in range(TILES):
         merge(last, tile)
 
@@ -400,6 +454,9 @@
             pltpu.VMEM((heads_here, HEAD_DIM, tokens), noisy.dtype),
             pltpu.VMEM((heads_here, 2, tokens), jnp.float32),
             pltpu.VMEM((heads_here, tokens, HEAD_DIM), noisy.dtype),
+            pltpu.VMEM((tokens, tokens), jnp.float32),
+            pltpu.VMEM((tokens, tokens), jnp.float32),
+            pltpu.VMEM((tokens, tokens), noisy.dtype),
             dma((3, peers)), dma((3, peers)),
             dma((2, heads_here * 2 * SPLIT)), dma((2, heads_here * 2 * SPLIT)),
             dma((heads_here,)), dma((heads_here,)),

time: 69.9 us -> 66.2 us (0.947)
  Pallas kernels: 67.6 us -> 64 us
    pallas_call x1, Pallas kernels: 67.6 us -> 64 us  [on_device(): pl.pallas_call(functools.partial(kernel, groups, heads_axis), out_shape=j...]
where the time goes in v4:
time: 66.2 us; the launch traced here: 66 us
  Pallas kernels  64 us (97%)
  local copies, waits for them, and re-layouts  2.06 us (3%)
    pallas_call x1, Pallas kernels, on_device(): pl.pallas_call(functools.partial(kernel, groups, heads_axis), out_shape=j...  64 us
    unnamed x1, local copies, waits for them, and re-layouts  2.06 us

profile of v4, /device:TPU:1, one launch (start us, length us, event | category | flops | bytes accessed | tf_op | source)
XLA Modules:
  0.0 66.0 jit_solution(10028966861936050050)
XLA Ops:
  0.0 64.0 %shard_map.46 = bf16[128,3072]{1,0:T(8,128)(2,1)} custom-call(bf16[3,128,3072]{2,1,0:T(8,128)(2,1)} %bitcast.4, bf16[1024,3,2,128]{3,2,1,0:T(2,128)(2,1)} %bitcast.5, s32[4]{0:T(128)} %lengths_ref.1, s32[4,4]{1,0:T(4,128)} %pattern_ref.1), custom_call_target="tpu_custom_call" | custom-call | flops 8053063680 | bytes 3145728 | tf_op jit(solution)/shard_map/pallas_call | solution.py:440
  64.0 2.1 %copy.6 = bf16[128,3072]{1,0:T(8,128)(2,1)} copy(bf16[128,3072]{1,0:T(8,128)(2,1)} %shard_map.46) | data formatting | bytes 1572864

commit v5 on v4

--- a/solution.py
+++ b/solution.py
@@ -81,6 +81,7 @@
     far = group - column + (ROW - 1) - column
     below = lax.rem(group + ROW, groups)
     above = lax.rem(group + groups - ROW, groups)
+    first_row, sends_below = group < ROW, group < groups - ROW
     peers = [lax.rem(head + k, heads_axis) for k in range(1, heads_axis)]
 
     mine_ok = validity(group, lengths_ref, pattern_ref)
@@ -144,6 +145,10 @@
             keyval.at[(OWN, *at)], keyval.at[(ABOVE, *at)], clean_send.at[0, i], clean_recv.at[0, i], below, head
         )
 
+    def fill_copy(i):
+        at = piece(i)
+        return pltpu.make_async_copy(keyval.at[(OWN, *at)], keyval.at[(ABOVE, *at)], clean_recv.at[0, i])
+
     def across_copy(i, relay):
         at = piece(i)
         src = keyval.at[(ABOVE if relay else OWN, *at)]
@@ -181,8 +186,17 @@
     barrier = pltpu.get_barrier_semaphore()
     for to in peers:
         pl.semaphore_signal(barrier, inc=1, device_id=(group, to), device_id_type=MESH)
-    for to in (near, far, below, above):
+    for to in (near, far):
         pl.semaphore_signal(barrier, inc=1, device_id=(to, head), device_id_type=MESH)
+
+    @pl.when(sends_below)
+    def _():
+        pl.semaphore_signal(barrier, inc=1, device_id=(below, head), device_id_type=MESH)
+
+    @pl.when(~first_row)
+    def _():
+        pl.semaphore_signal(barrier, inc=1, device_id=(above, head), device_id_type=MESH)
+
     for h in range(heads_here):
         paired_copy(h).start()
     for which in range(3):
@@ -192,16 +206,25 @@
         paired_copy(h).wait()
         part_pairs(h)
         if h == 0:
-            pl.semaphore_wait(barrier, len(peers) + 4)
+            pl.semaphore_wait(barrier, len(peers) + 2 + jnp.where(sends_below, 1, 0) + jnp.where(first_row, 0, 1))
             for k in others:
                 noisy_copy(0, k).start()
-        for i in pieces:
-            if i // (2 * SPLIT) == h:
+        of_head = [i for i in pieces if i // (2 * SPLIT) == h]
+
+        @pl.when(sends_below)
+        def _():
+            for i in of_head:
                 above_copy(i).start()
 
-                @pl.when(column < 2)
-                def _():
-                    across_copy(i, False).start()
+        @pl.when(first_row)
+        def _():
+            for i in of_head:
+                fill_copy(i).start()
+
+        @pl.when(column < 2)
+        def _():
+            for i in of_head:
+                across_copy(i, False).start()
 
     accum[...] = jnp.zeros_like(accum)
     total[...] = jnp.zeros_like(total)
@@ -424,8 +447,12 @@
             out_copy(h, peers[k]).wait()
             noisy_copy(h, k).wait_send()
     for i in pieces:
-        above_copy(i).wait_send()
         across_copy(i, False).wait_send()
+
+    @pl.when(sends_below)
+    def _():
+        for i in pieces:
+            above_copy(i).wait_send()
 
 
 def on_device(groups, heads_axis, noisy_qkv, clean_kv, video_lengths, pattern):

time: 66.2 us -> 63.1 us (0.953)
  the two profiles are of different devices: /device:TPU:1 before, /device:TPU:123 now
where the time goes in v5:
time: 63.1 us; the launch traced here: 62.9 us
  Pallas kernels  60.8 us (96%)
  local copies, waits for them, and re-layouts  2.06 us (3%)
    pallas_call x1, Pallas kernels, on_device(): pl.pallas_call(functools.partial(kernel, groups, heads_axis), out_shape=j...  60.8 us
    unnamed x1, local copies, waits for them, and re-layouts  2.06 us

profile of v5, /device:TPU:123, one launch (start us, length us, event | category | flops | bytes accessed | tf_op | source)
XLA Modules:
  0.0 62.9 jit_solution(17459618595195850360)
XLA Ops:
  0.0 60.8 %shard_map.46 = bf16[128,3072]{1,0:T(8,128)(2,1)} custom-call(bf16[3,128,3072]{2,1,0:T(8,128)(2,1)} %bitcast.4, bf16[1024,3,2,128]{3,2,1,0:T(2,128)(2,1)} %bitcast.5, s32[4]{0:T(128)} %lengths_ref.1, s32[4,4]{1,0:T(4,128)} %pattern_ref.1), custom_call_target="tpu_custom_call" | custom-call | flops 8053063680 | bytes 3145728 | tf_op jit(solution)/shard_map/pallas_call | solution.py:467
  60.8 2.1 %copy.6 = bf16[128,3072]{1,0:T(8,128)(2,1)} copy(bf16[128,3072]{1,0:T(8,128)(2,1)} %shard_map.46) | data formatting | bytes 1572864

commit v6 on v5

--- a/solution.py
+++ b/solution.py
@@ -35,7 +35,7 @@
     (None, PARTNER, 2),
     (ACROSS, PARTNER, 2),
 )
-PASS_ON = {0: (2, 3), 1: (4,), 3: (5,), 4: (6, 7), 5: (8,), 7: (9,), 8: (10,), 11: (11,)}
+PASS_ON = {0: (2, 3), 1: (4,), 3: (5,), 4: (6, 7), 5: (8,), 6: (9,), 8: (10,), 11: (11,)}
 HAND_OVER_AFTER = {3: 0, 7: 1}
 MERGE_AFTER = {9: 0}
 
@@ -420,6 +420,7 @@
     peak[PARTNER, last] = now
     total[PARTNER, last] = total[PARTNER, last] * factor + jnp.sum(expo, axis=0, keepdims=True)
     following = begin_at(ABOVE, MINE, last, odd_scores)
+    largest = begin_at(ACROSS, MINE, last, even_scores)
     take_across(last, 1)
     for tile in range(TILES):
         at = tile_of(tile)
@@ -430,7 +431,6 @@
         n = tokens // TILES
         accum[PARTNER, last, :, at] = accum[PARTNER, last, :, at] * factor[:, tile * n:(tile + 1) * n] + added
         hand_over(last, tile)
-    largest = begin_at(ACROSS, MINE, last, even_scores)
     weigh(ABOVE, MINE, last, mine_ok[3], every, odd_scores[...], following)
     merge(1)
     keep = (mine_ok[0] & (odd == 0)) | (mine_ok[2] & (odd == 1))

time: 63.1 us -> 62.8 us (level)
  the two profiles are of different devices: /device:TPU:123 before, /device:TPU:97 now
where the time goes in v6:
time: 62.8 us; the launch traced here: 62.7 us
  Pallas kernels  60.6 us (96%)
  local copies, waits for them, and re-layouts  2.06 us (3%)
    pallas_call x1, Pallas kernels, on_device(): pl.pallas_call(functools.partial(kernel, groups, heads_axis), out_shape=j...  60.6 us
    unnamed x1, local copies, waits for them, and re-layouts  2.06 us

profile of v6, /device:TPU:97, one launch (start us, length us, event | category | flops | bytes accessed | tf_op | source)
XLA Modules:
  0.0 62.7 jit_solution(16884231990387008861)
XLA Ops:
  0.0 60.6 %shard_map.46 = bf16[128,3072]{1,0:T(8,128)(2,1)} custom-call(bf16[3,128,3072]{2,1,0:T(8,128)(2,1)} %bitcast.4, bf16[1024,3,2,128]{3,2,1,0:T(2,128)(2,1)} %bitcast.5, s32[4]{0:T(128)} %lengths_ref.1, s32[4,4]{1,0:T(4,128)} %pattern_ref.1), custom_call_target="tpu_custom_call" | custom-call | flops 8053063680 | bytes 3145728 | tf_op jit(solution)/shard_map/pallas_call | solution.py:467
  60.6 2.1 %copy.6 = bf16[128,3072]{1,0:T(8,128)(2,1)} copy(bf16[128,3072]{1,0:T(8,128)(2,1)} %shard_map.46) | data formatting | bytes 1572864

commit v7 on v6

--- a/solution.py
+++ b/solution.py
@@ -207,8 +207,6 @@
         part_pairs(h)
         if h == 0:
             pl.semaphore_wait(barrier, len(peers) + 2 + jnp.where(sends_below, 1, 0) + jnp.where(first_row, 0, 1))
-            for k in others:
-                noisy_copy(0, k).start()
         of_head = [i for i in pieces if i // (2 * SPLIT) == h]
 
         @pl.when(sends_below)
@@ -225,6 +223,10 @@
         def _():
             for i in of_head:
                 across_copy(i, False).start()
+
+        if h == 0:
+            for k in others:
+                noisy_copy(0, k).start()
 
     accum[...] = jnp.zeros_like(accum)
     total[...] = jnp.zeros_like(total)

time: 62.8 us -> 62.8 us (level)
  no operation moved by 1% of the time
where the time goes in v7:
time: 62.8 us; the launch traced here: 62.7 us
  Pallas kernels  60.6 us (96%)
  local copies, waits for them, and re-layouts  2.06 us (3%)
    pallas_call x1, Pallas kernels, on_device(): pl.pallas_call(functools.partial(kernel, groups, heads_axis), out_shape=j...  60.6 us
    unnamed x1, local copies, waits for them, and re-layouts  2.06 us

profile of v7, /device:TPU:97, one launch (start us, length us, event | category | flops | bytes accessed | tf_op | source)
XLA Modules:
  0.0 62.7 jit_solution(12306212001447427146)
XLA Ops:
  0.0 60.6 %shard_map.46 = bf16[128,3072]{1,0:T(8,128)(2,1)} custom-call(bf16[3,128,3072]{2,1,0:T(8,128)(2,1)} %bitcast.4, bf16[1024,3,2,128]{3,2,1,0:T(2,128)(2,1)} %bitcast.5, s32[4]{0:T(128)} %lengths_ref.1, s32[4,4]{1,0:T(4,128)} %pattern_ref.1), custom_call_target="tpu_custom_call" | custom-call | flops 8053063680 | bytes 3145728 | tf_op jit(solution)/shard_map/pallas_call | solution.py:469
  60.6 2.1 %copy.6 = bf16[128,3072]{1,0:T(8,128)(2,1)} copy(bf16[128,3072]{1,0:T(8,128)(2,1)} %shard_map.46) | data formatting | bytes 1572864
